TPU v7x, 128 devices: a whole 4x4x4 slice. The times are simulated.
128 devices in a mesh: exp: 64 (over z, y, x), grp: 2 (over core).
Axes of the slice: x: 4, y: 4, z: 4, core: 2. Of those that a mesh axis runs over, the one named last changes fastest.
Arguments:
- tokens: bfloat16 [65536, 3584], P(('exp', 'grp')), may hold values from -6 to 6
- routes: int32 [65536, 1], P(('exp', 'grp')), may hold values from 0 to 63; in each aligned block of 512 rows (0 to 511, 512 to 1023, ...) at most 12 rows name the same one
- gate_prob: float32 [65536, 1], P(('exp', 'grp')), may hold values from 0.1 to 1
- w_gate: bfloat16 [64, 3584, 1024], P('exp', None, 'grp'), may hold values from -0.09375 to 0.09375
- w_up: bfloat16 [64, 3584, 1024], P('exp', None, 'grp'), may hold values from -0.09375 to 0.09375
- hidden_grad: bfloat16 [64, 1536, 1024], P('exp', None, 'grp'), may hold values from -0.1875 to 0.1875
Outputs:
- grad_gate: bfloat16 [64, 3584, 1024], P('exp', None, 'grp')
- grad_up: bfloat16 [64, 3584, 1024], P('exp', None, 'grp')
- prob_grad: float32 [65536, 1], P(('exp', 'grp'))
Inputs may be any that keep to these rules, and one draw needn't show every extreme that they name: Among the 512 tokens of one device at most 12 routes go to any one expert, and in every draw some device sends exactly 12 to some expert.
All inputs are finite; a program needn't handle non-finite values.
Results may differ from a plain program's by a relative error of at most 0.0056.
Values may be sent and summed in bfloat16 or wider, within the bound.
A program may use at most 128 MiB of HBM per device.

v0:
```python
import jax
import jax.numpy as jnp
from jax import lax
from jax.sharding import PartitionSpec as P


def route_targets(routes, expert_count, capacity):
    flat_ids = routes.reshape(-1)
    expert_list = jnp.arange(expert_count, dtype=jnp.int32)
    member = (flat_ids[:, None] == expert_list[None, :]).astype(jnp.int32)
    earlier = jnp.cumsum(member, axis=0) - member
    position = jnp.sum(earlier * member, axis=1)
    return flat_ids * capacity + position


def project(rows, weight_gate, weight_up):
    gate_proj = jnp.dot(rows, weight_gate, preferred_element_type=jnp.float32)
    up_proj = jnp.dot(rows, weight_up, preferred_element_type=jnp.float32)
    return (gate_proj, up_proj)


def finish_slots(rows, probs, cot_values, gate_proj, up_proj):
    sigmoid_gate = jax.nn.sigmoid(gate_proj)
    activated = gate_proj * sigmoid_gate
    slot_grad = jnp.sum(activated * up_proj * cot_values, axis=1)
    scaled = probs.astype(jnp.float32)[:, None] * cot_values
    up_term = (scaled * activated).astype(jnp.bfloat16)
    gate_term = (scaled * up_proj * sigmoid_gate * (1.0 + gate_proj * (1.0 - sigmoid_gate))).astype(
        jnp.bfloat16
    )
    contract = (((0,), (0,)), ((), ()))
    grad_g = lax.dot_general(rows, gate_term, contract, preferred_element_type=jnp.float32)
    grad_u = lax.dot_general(rows, up_term, contract, preferred_element_type=jnp.float32)
    return (grad_g, grad_u, slot_grad)


def slot_terms(rows, probs, cot_values, weight_gate, weight_up):
    gate_proj, up_proj = project(rows, weight_gate, weight_up)
    return finish_slots(rows, probs, cot_values, gate_proj, up_proj)


def body(tokens, routes, gate_prob, w_gate, w_up, hidden_grad):
    expert_count = lax.axis_size("exp")
    group_count = lax.axis_size("grp")
    route_count = routes.shape[1]
    features = tokens.shape[1]
    slot_total = hidden_grad.shape[1]
    capacity = slot_total // (group_count * expert_count)
    targets = route_targets(routes, expert_count, capacity)
    places = jnp.arange(expert_count * capacity, dtype=jnp.int32)
    selected = places[:, None] == targets[None, :]
    route_rows = jnp.repeat(tokens, route_count, axis=0)
    send_rows = jnp.dot(
        selected.astype(jnp.bfloat16), route_rows, preferred_element_type=jnp.float32
    ).astype(jnp.bfloat16)
    send_prob = jnp.sum(jnp.where(selected, gate_prob.reshape(-1)[None, :], 0.0), axis=1).astype(
        jnp.bfloat16
    )
    send_rows = send_rows.reshape(expert_count, capacity, features)
    send_prob = send_prob.reshape(expert_count, capacity)
    weight_gate = w_gate[0]
    weight_up = w_up[0]
    cot_all = hidden_grad[0].astype(jnp.float32)
    arrived_rows, arrived_prob = (
        lax.all_to_all(send_rows, "exp", split_axis=0, concat_axis=0, tiled=True),
        lax.all_to_all(send_prob, "exp", split_axis=0, concat_axis=0, tiled=True),
    )
    local_rows = arrived_rows.reshape(expert_count * capacity, features)
    local_prob = arrived_prob.reshape(expert_count * capacity)
    all_rows, all_prob = (
        lax.all_gather(local_rows, "grp", axis=0, tiled=True),
        lax.all_gather(local_prob, "grp", axis=0, tiled=True),
    )
    grad_g, grad_u, partial_sums = slot_terms(all_rows, all_prob, cot_all, weight_gate, weight_up)
    own_sums = lax.psum_scatter(partial_sums, "grp", scatter_dimension=0, tiled=True)
    returned = lax.all_to_all(
        own_sums.reshape(expert_count, capacity), "exp", split_axis=0, concat_axis=0, tiled=True
    )
    prob_values = jnp.sum(jnp.where(selected, returned.reshape(-1)[:, None], 0.0), axis=0)
    prob_grad = prob_values.reshape(tokens.shape[0], route_count)
    return (grad_g.astype(jnp.bfloat16)[None], grad_u.astype(jnp.bfloat16)[None], prob_grad)


def solution(mesh):
    in_specs = (
        P(("exp", "grp"), None),
        P(("exp", "grp"), None),
        P(("exp", "grp"), None),
        P("exp", None, "grp"),
        P("exp", None, "grp"),
        P("exp", None, "grp"),
    )
    out_specs = (P("exp", None, "grp"), P("exp", None, "grp"), P(("exp", "grp"), None))
    return jax.shard_map(body, mesh=mesh, in_specs=in_specs, out_specs=out_specs, check_vma=False)
```

profile of v0, /device:TPU:1, one launch (start us, length us, event | category | flops | bytes accessed | tf_op | source)
XLA Modules:
  0.0 252.0 jit_solution(6596642602984460463)
XLA Ops:
  7.2 0.0 all-gather.3.cloned.1.call-start
  7.2 0.7 fusion.26
  7.9 1.2 reduce-window.6
  9.1 0.2 slice_reduce_fusion
  9.4 0.8 fusion.25
  10.2 0.7 multiply_add_fusion
  10.9 6.8 %convolution_convert_fusion = bf16[768,3584]{1,0:T(8,128)(2,1)} fusion(bf16[512,3584]{1,0:T(8,128)(2,1)} %param.6, s32[512]{0:T(512)S(1)} %multiply_add_fusion), kind=kOutput, calls=%fused_computation | convolution fusion | flops 2821718016 | bytes 9177088 | tf_op jit(solution)/shard_map/dot_general | solution.py:53
  17.6 9.3 %reshape.73 = bf16[64,12,3584]{2,1,0:T(8,128)(2,1)} reshape(bf16[768,3584]{1,0:T(8,128)(2,1)} %convolution_convert_fusion) | data formatting | bytes 11010048 | tf_op jit(solution)/shard_map/reshape | solution.py:59
  26.9 97.2 %all_to_all.20 = bf16[64,12,3584]{2,1,0:T(8,128)(2,1)} all-to-all(bf16[64,12,3584]{2,1,0:T(8,128)(2,1)} %reshape.73), channel_id=1, replica_groups=mesh['exp'=64,'grp'=2] {'exp'}, dimensions={0} | all-to-all | bytes 11010048 | tf_op jit(solution)/shard_map/all_to_all | solution.py:65
  124.1 9.4 %reshape.74 = bf16[768,3584]{1,0:T(8,128)(2,1)} reshape(bf16[64,12,3584]{2,1,0:T(8,128)(2,1)} %all_to_all.20) | data formatting | bytes 11010048 | tf_op jit(solution)/shard_map/reshape | solution.py:68
  133.5 0.0 all-gather.3.cloned.1.call-update
  133.5 1.4 copy-done
  134.9 0.7 copy.18
  135.6 0.6 dynamic-slice
  136.8 21.7 %all-gather.3.cloned.1.call-done = bf16[1536,3584]{1,0:T(8,128)(2,1)} async-done(((bf16[768,3584]{1,0:T(8,128)(2,1)}), bf16[1536,3584]{1,0:T(8,128)(2,1)}) %all-gather.3.cloned.1.call-update) | async-done | bytes 11010064 | tf_op jit(solution)/shard_map/all_gather | solution.py:71
  158.5 11.1 %fusion.4 = f32[1536,512]{0,1:T(8,128)} fusion(bf16[1536,3584]{1,0:T(8,128)(2,1)} %all-gather.3.cloned.1.call-done, bf16[1,3584,512]{2,1,0:T(8,128)(2,1)} %param.9), kind=kOutput, calls=%fused_computation.9 | convolution fusion | flops 5637144576 | bytes 17825792 | tf_op jit(solution)/shard_map/dot_general | solution.py:17
  169.6 9.9 %fusion.12 = (f32[1536]{0:T(1024)S(1)}, f32[1536,512]{0,1:T(8,128)}) fusion(bf16[1,1536,512]{1,2,0:T(8,128)(2,1)S(1)} %copy.18, f32[1536,512]{0,1:T(8,128)} %fusion.4, bf16[1536,3584]{1,0:T(8,128)(2,1)S(1)} %copy-done.2, bf16[1,3584,512]{2,1,0:T(8,128)(2,1)} %param.10), kind=kOutput, calls=%fused_computation.17 | convolution fusion | flops 5643434496 | bytes 22550528 | tf_op jit(solution)/shard_map/dot_general | solution.py:18
  179.5 2.5 all-reduce
  181.9 0.1 dynamic-slice.1
  182.0 0.1 all_to_all.15
  182.1 18.3 %all_to_all.21 = f32[64,1,12]{2,1,0:T(1,128)S(1)} all-to-all(f32[64,1,12]{2,1,0:T(1,128)S(1)} %bitcast.53), channel_id=1, replica_groups=mesh['exp'=64,'grp'=2] {'exp'}, dimensions={0} | all-to-all | bytes 6144 | tf_op jit(solution)/shard_map/all_to_all | solution.py:76
  200.5 0.5 broadcast.43
  201.0 0.7 reduce.8
  201.7 0.1 broadcast_in_dim.41
  201.8 1.0 select_reduce_fusion
  202.8 0.1 convert_element_type.60
  203.0 12.9 %all_to_all.22 = bf16[64,1,12]{2,1,0:T(2,128)(2,1)S(1)} all-to-all(bf16[64,1,12]{2,1,0:T(2,128)(2,1)S(1)} %convert_element_type.60), channel_id=1, replica_groups=mesh['exp'=64,'grp'=2] {'exp'}, dimensions={0} | all-to-all | bytes 3072 | tf_op jit(solution)/shard_map/all_to_all | solution.py:66
  215.8 0.1 reduce.1
  215.9 0.1 reshape.78
  216.1 4.5 %all-gather = bf16[2,1,768]{2,1,0:T(2,128)(2,1)S(1)} all-gather(bf16[1,1,768]{2,1,0:T(2,128)(2,1)S(1)} %reshape.78), channel_id=1, replica_groups=mesh['exp'=64,'grp'=2] {'grp'}, dimensions={0}, use_global_device_ids=true | all-gather | bytes 4608 | tf_op jit(solution)/shard_map/all_gather | solution.py:72
  220.7 12.4 %fusion.1 = bf16[1,3584,512]{2,1,0:T(8,128)(2,1)} fusion(bf16[1536,3584]{1,0:T(8,128)(2,1)} %all-gather.3.cloned.1.call-done, bf16[1,1536,512]{1,2,0:T(8,128)(2,1)S(1)} %copy.18, f32[1536]{0:T(1024)S(1)} %reshape.80, f32[1536,512]{0,1:T(8,128)} %fusion.4), kind=kOutput, calls=%fused_computation.4 | convolution fusion | flops 5645271040 | bytes 19404800 | tf_op jit(solution)/shard_map/dot_general | solution.py:33
  233.1 12.0 %fusion = bf16[1,3584,512]{2,1,0:T(8,128)(2,1)} fusion(bf16[1536,3584]{1,0:T(8,128)(2,1)} %all-gather.3.cloned.1.call-done, f32[1536,512]{0,1:T(8,128)S(1)} %copy-done.5, f32[1536,512]{0,1:T(8,128)S(1)} %copy-done.4, bf16[1,1536,512]{1,2,0:T(8,128)(2,1)S(1)} %copy.18, f32[1536]{0:T(1024)S(1)} %reshape.80), kind=kOutput, calls=%fused_computation.3 | convolution fusion | flops 5648416768 | bytes 22550528 | tf_op jit(solution)/shard_map/dot_general | solution.py:32
  (15 shorter events, 0.1 us)
Async XLA Ops:
  7.2 151.3 %all-gather.3.cloned.1.call-start = ((), (), s32[]{:S(2)}) async-start(), calls=%async_computation.3 | async-start | bytes 16515072 | tf_op jit(solution)/shard_map/all_gather | solution.py:71
  133.5 1.4 copy-start
  133.5 2.1 copy-start.3
  158.5 11.1 %copy-start.2 = (bf16[1536,3584]{1,0:T(8,128)(2,1)S(1)}, bf16[1536,3584]{1,0:T(8,128)(2,1)}, u32[]{:S(2)}) copy-start(bf16[1536,3584]{1,0:T(8,128)(2,1)} %all-gather.3.cloned.1.call-done) | copy-start | bytes 33030148
  169.6 32.2 %copy-start.1 = (f32[512,1]{0,1:T(1,128)S(1)}, f32[512,1]{0,1:T(1,128)}, u32[]{:S(2)}) copy-start(f32[512,1]{0,1:T(1,128)} %param.8) | copy-start | bytes 6148
  220.7 12.5 %copy-start.4 = (f32[1536,512]{0,1:T(8,128)S(1)}, f32[1536,512]{0,1:T(8,128)}, u32[]{:S(2)}) copy-start(f32[1536,512]{0,1:T(8,128)} %fusion.4) | copy-start | bytes 9437188
  220.7 12.5 %copy-start.5 = (f32[1536,512]{0,1:T(8,128)S(1)}, f32[1536,512]{0,1:T(8,128)}, u32[]{:S(2)}) copy-start(f32[1536,512]{0,1:T(8,128)} %get-tuple-element.6) | copy-start | bytes 9437188
Sparse Core Ops, SparseCore 0:
  133.6 24.8 all-gather.2
where the time goes:
time: 253 us; the launch traced here: 252 us
  blocking collectives  135 us (53%)
  matrix products  52.1 us (21%)
  local copies, waits for them, and re-layouts  22.6 us (9%)
  waiting for transfers between devices  21.7 us (9%)
  between operations  14.8 us (6%)
  other arithmetic  5.31 us (2%)
    all_to_all x1, blocking collectives, body(): lax.all_to_all(send_rows, 'exp', split_axis=0, concat_axis=0, tiled=True)  97.2 us
    all_gather x1, waiting for transfers between devices, body(): lax.all_gather(local_rows, 'grp', axis=0, tiled=True)  21.7 us
    all_to_all x1, blocking collectives, body(): lax.all_to_all(own_sums.reshape(expert_count, capacity), 'exp', split_axi...  18.3 us
    all_to_all x1, blocking collectives, body(): lax.all_to_all(send_prob, 'exp', split_axis=0, concat_axis=0, tiled=True)  12.9 us
    dot_general x1, matrix products, finish_slots(): lax.dot_general(rows, up_term, contract, preferred_element_type=jnp.float32)  12.4 us
    dot_general x1, matrix products, finish_slots(): lax.dot_general(rows, gate_term, contract, preferred_element_type=jnp.flo...  12 us
    dot_general x1, matrix products, project(): gate_proj = jnp.dot(rows, weight_gate, preferred_element_type=jnp.float32)  11.1 us
    dot_general x1, matrix products, project(): up_proj = jnp.dot(rows, weight_up, preferred_element_type=jnp.float32)  9.87 us
  transfers between devices with their start and end apart: 1, of which 1 were waited for; matrix products, arithmetic and copies ran while one was open for 1% of the time, Pallas kernels for 0%

commit v1 on v0

v1 whole, which is shorter than its diff:
```python
import jax
import jax.numpy as jnp
from jax import lax
from jax.experimental import pallas as pl
from jax.experimental.pallas import tpu as pltpu
from jax.sharding import PartitionSpec as P

BF16, F32, I32 = jnp.bfloat16, jnp.float32, jnp.int32
MESH = pl.DeviceIdType.MESH
HIGH = lax.Precision.HIGHEST

D = 3584
HALF = 512
TOK = 512
N_EXP = 64
CAP = 12
PART = 896
MAIN = 3 * PART
STEPS = 8
ROWS = 192
GROUP = 48
TILE = 512
CHUNKS = ((0, 8), (8, 24), (32, 32))


def kernel(
    tok_hbm, routes_ref, prob_ref, wg_hbm, wu_hbm, hg_hbm,
    gg_hbm, gu_hbm, pg_ref,
    tok, send, recv, rows, wg, wu, hg, acc, terms, stage, member_ref,
    prs, pr_own, pr_part, ret_out, ret_own, ret_part,
    send_sem, recv_sem, prs_sem, prr_sem, rets_sem, retr_sem,
    fwds_sem, fwdr_sem, part_sem, load_sem, out_sem, self_sem,
):
    me = lax.axis_index("exp")
    g = lax.axis_index("grp")
    z, y, x = me // 16, (me // 4) % 4, me % 4
    partner = {"exp": me, "grp": 1 - g}

    def target(k, m, dx):
        dz, dy = k // 4 + 2 * m, k % 4 + 2 * m
        return ((z + dz) % 4) * 16 + ((y + dy) % 4) * 4 + (x + dx) % 4

    def group_of(k, m):
        dz, dy = k // 4 + 2 * m, k % 4 + 2 * m
        return ((z + 8 - dz) % 4) * 4 + (y + 8 - dy) % 4

    barrier = pltpu.get_barrier_semaphore()

    @pl.loop(1, N_EXP)
    def _(i):
        pl.semaphore_signal(barrier, inc=1, device_id={"exp": (me + i) % N_EXP, "grp": g}, device_id_type=MESH)

    pl.semaphore_signal(barrier, inc=1, device_id=partner, device_id_type=MESH)

    def columns(p):
        return pl.ds(p * PART, PART)

    tok_loads = [pltpu.make_async_copy(tok_hbm.at[:, columns(p)], tok.at[:, columns(p)], load_sem.at[p]) for p in range(4)]
    for p in (3, 0, 1, 2):
        tok_loads[p].start()
    w_loads = [
        pltpu.make_async_copy(wg_hbm.at[0], wg, load_sem.at[4]),
        pltpu.make_async_copy(wu_hbm.at[0], wu, load_sem.at[5]),
        pltpu.make_async_copy(hg_hbm.at[0], hg, load_sem.at[6]),
    ]
    for load in w_loads:
        load.start()

    r = lax.broadcasted_iota(I32, (N_EXP, TOK), 0)
    rk, rm, rx = r >> 3, (r >> 2) & 1, r & 3
    expert = ((z + (rk >> 2) + 2 * rm) & 3) * 16 + ((y + (rk & 3) + 2 * rm) & 3) * 4 + ((x + rx) & 3)
    member = jnp.where(expert == routes_ref[...], 1.0, 0.0).astype(F32)
    member_ref[...] = member
    before = lax.broadcasted_iota(I32, (TOK, TOK), 0) < lax.broadcasted_iota(I32, (TOK, TOK), 1)
    earlier = jnp.dot(member.astype(BF16), jnp.where(before, 1.0, 0.0).astype(BF16), preferred_element_type=F32)
    pos = jnp.sum(member * earlier, axis=0, keepdims=True).astype(I32)
    rank = jnp.sum(member * r.astype(F32), axis=0, keepdims=True).astype(I32)
    main_row = rank * 16 + ((12 * x + pos) & 15)
    tail_row = rank * 8 + (pos & 3)
    tail_part = pos >> 2
    tail_first = (12 * x + 12) % 16
    i16 = lax.broadcasted_iota(I32, (1, 16, PART), 1)
    tail_mask = (i16 >= tail_first) & (i16 < tail_first + 4)

    lane_slot = lax.broadcasted_iota(I32, (128, TOK), 0)
    prob_at = jnp.where(lane_slot == pos, prob_ref[...], 0.0).astype(BF16)
    prs[:, 0, :] = lax.dot_general(member.astype(BF16), prob_at, (((1,), (1,)), ((), ())), preferred_element_type=F32)

    def send_copy(k, m, dx):
        rk_ = k * 8 + m * 4 + dx
        slot = (k * 2 + m) * 4 + x
        return pltpu.make_async_remote_copy(
            send.at[rk_], recv.at[slot], send_sem.at[rk_], recv_sem.at[slot],
            device_id={"exp": target(k, m, dx), "grp": g}, device_id_type=MESH)

    def prob_copy(k, m, dx):
        rk_ = k * 8 + m * 4 + dx
        slot = (k * 2 + m) * 4 + x
        return pltpu.make_async_remote_copy(
            prs.at[rk_], pr_own.at[slot], prs_sem.at[rk_], prr_sem.at[slot],
            device_id={"exp": target(k, m, dx), "grp": g}, device_id_type=MESH)

    def return_copy(k, m, sx):
        idx = k * 8 + m * 4 + sx
        slot = k * 8 + m * 4 + (x + 4 - sx) % 4
        return pltpu.make_async_remote_copy(
            ret_out.at[idx], ret_own.at[slot], rets_sem.at[idx], retr_sem.at[slot],
            device_id={"exp": group_of(k, m) * 4 + sx, "grp": g}, device_id_type=MESH)

    self_rows = pltpu.make_async_copy(send.at[0], recv.at[x], self_sem.at[0])
    self_prob = pltpu.make_async_copy(prs.at[0], pr_own.at[x], self_sem.at[1])
    self_ret = pltpu.make_async_copy(ret_out.at[x], ret_own.at[0], self_sem.at[2])

    def build(first, count):
        hit = lax.broadcasted_iota(I32, (16 * count, TOK), 0) + 16 * first == main_row
        pick = jnp.where(hit, 1.0, 0.0).astype(BF16)
        it = lax.broadcasted_iota(I32, (8 * count, TOK), 0) + 8 * first
        picks = []
        for p in range(3):
            own = jnp.where(tail_part == p, tail_row, -100)
            picks.append(jnp.where((it == own) | (it == own + 4), 1.0, 0.0).astype(BF16))
        if first == 0:
            tok_loads[3].wait()
        tails = jnp.dot(jnp.concatenate(picks, axis=0), tok[:, MAIN:], preferred_element_type=F32)
        for p in range(3):
            if first == 0:
                tok_loads[p].wait()
            main = jnp.dot(pick, tok[:, p * PART:(p + 1) * PART], preferred_element_type=F32)
            tail = tails[p * 8 * count:(p + 1) * 8 * count].reshape(count, 8, PART)
            both = jnp.concatenate([tail, tail], axis=1)
            block = jnp.where(tail_mask, both, main.reshape(count, 16, PART)).astype(BF16)
            send[first:first + count, :, p * PART:(p + 1) * PART] = block

    for first, count in CHUNKS:
        build(first, count)
        if first == 0:
            pl.semaphore_wait(barrier, N_EXP)
            self_rows.start()
            self_prob.start()

        @pl.loop(max(first, 1), first + count)
        def _(i):
            m = i % 2
            send_copy(i // 8, m, ((i % 8) // 2 + 2 * m) % 4).start()

        if first == 0:
            @pl.loop(1, N_EXP)
            def _(i):
                prob_copy(i // 8, (i // 4) % 2, i % 4).start()

    acc[...] = jnp.zeros_like(acc)

    @pl.loop(1, N_EXP)
    def _(i):
        k, m, dx = i // 8, (i // 4) % 2, i % 4
        slot = (k * 2 + m) * 4 + (x + 4 - dx) % 4
        pltpu.make_async_remote_copy(
            prs.at[0], pr_own.at[slot], prs_sem.at[0], prr_sem.at[slot], device_id=partner, device_id_type=MESH).wait_recv()

    self_prob.wait()
    prob_forward = pltpu.make_async_remote_copy(
        pr_own, pr_part, part_sem.at[0], part_sem.at[1], device_id=partner, device_id_type=MESH)
    prob_forward.start()
    prob_forward.wait_recv()
    for load in w_loads:
        load.wait()

    def forward_copy(k):
        return pltpu.make_async_remote_copy(
            rows.at[k, g], rows.at[k, g], fwds_sem.at[k], fwdr_sem.at[k], device_id=partner, device_id_type=MESH)

    low = lax.broadcasted_iota(I32, (8, PART), 0) < 4

    def unpack(k, m):
        base = (k * 2 + m) * 4

        def half(s, h, p):
            return recv[base + s, :, p * PART:(p + 1) * PART].astype(F32)[8 * h:8 * h + 8]

        def put(t, p, lo, hi):
            rows[k, g, m * GROUP + 16 * t:m * GROUP + 16 * t + 16, p * PART:(p + 1) * PART] = jnp.concatenate(
                [lo, hi], axis=0).astype(BF16)

        for p in range(3):
            put(0, p, half(0, 0, p), jnp.where(low, half(0, 1, p), half(1, 1, p)))
            put(1, p, half(1, 0, p), half(2, 1, p))
            put(2, p, jnp.where(low, half(2, 0, p), half(3, 0, p)), half(3, 1, p))

        def quad(q):
            s, p = q // 3, q % 3
            at = 3 - s
            value = half(s, at // 2, p)
            return value if at % 2 == q % 2 else pltpu.roll(value, 4, 0)

        for t in range(3):
            lo, hi = (jnp.where(low, quad(4 * t + 2 * h), quad(4 * t + 2 * h + 1)) for h in range(2))
            put(t, 3, lo, hi)

    row16 = lax.broadcasted_iota(I32, (ROWS, 16), 0)
    at16 = lax.broadcasted_iota(I32, (ROWS, 16), 1) * CAP
    spread = jnp.where((row16 >= at16) & (row16 < at16 + CAP), 1.0, 0.0)
    row_t = lax.broadcasted_iota(I32, (16, ROWS), 1)
    at_t = lax.broadcasted_iota(I32, (16, ROWS), 0) * CAP
    spread_t = jnp.where((row_t >= at_t) & (row_t < at_t + CAP), 1.0, 0.0)
    row128 = lax.broadcasted_iota(I32, (ROWS, 128), 0)
    lane_hit = lax.broadcasted_iota(I32, (ROWS, 128), 1) == row128 - ((row128 * 5462) >> 16) * CAP

    def step(k):
        for m in range(2):
            for s in range(4):
                slot = (k * 2 + m) * 4 + s
                wait = pltpu.make_async_remote_copy(
                    send.at[0], recv.at[slot], send_sem.at[0], recv_sem.at[slot], device_id=partner, device_id_type=MESH)
                if m == 0:
                    own = (k == 0) & (x == s)
                    pl.when(own)(self_rows.wait)
                    pl.when(jnp.logical_not(own))(wait.wait_recv)
                else:
                    wait.wait_recv()
        unpack(k, 0)
        unpack(k, 1)
        forward = forward_copy(k)
        forward.start()
        own_p, other_p = pr_own[pl.ds(k * 8, 8), 0, :], pr_part[pl.ds(k * 8, 8), 0, :]
        first = g == 0
        probs = jnp.concatenate([jnp.where(first, own_p, other_p), jnp.where(first, other_p, own_p)], axis=0)
        probs = jnp.dot(spread.astype(BF16), probs.astype(BF16), preferred_element_type=F32)
        prob = jnp.sum(jnp.where(lane_hit, probs, 0.0), axis=1, keepdims=True)
        forward.wait_recv()
        total = jnp.zeros((ROWS, 1), F32)
        width = 256
        for n in range(HALF // width):
            sl = slice(n * width, (n + 1) * width)
            here = rows[k].reshape(ROWS, D)
            gate = jnp.dot(here, wg[:, sl], preferred_element_type=F32)
            up = jnp.dot(here, wu[:, sl], preferred_element_type=F32)
            pieces = [
                hg[pl.ds(pl.multiple_of(j * 768 + group_of(k, m) * GROUP, 16), GROUP), sl] for j in range(2) for m in range(2)]
            cot = jnp.concatenate(pieces, axis=0).astype(F32)
            sig = jax.nn.sigmoid(gate)
            act = gate * sig
            total = total + jnp.sum(act * up * cot, axis=1, keepdims=True)
            scaled = prob * cot
            terms[k, :, sl] = (scaled * up * sig * (1.0 + gate * (1.0 - sig))).astype(BF16)
            terms[k, :, HALF + n * width:HALF + (n + 1) * width] = (scaled * act).astype(BF16)
        by_source = jnp.dot(
            spread_t, jnp.where(lane_hit, total, 0.0), precision=HIGH, preferred_element_type=F32)
        ret_out[pl.ds(k * 8, 8), 0, :] = by_source[0:8]
        ret_out[pl.ds(k * 8, 8), 1, :] = by_source[8:16]
        for m in range(2):
            for s in range(4):
                copy = return_copy(k, m, s)
                if m == 0:
                    own = (k == 0) & (x == s)
                    pl.when(own)(self_ret.start)
                    pl.when(jnp.logical_not(own))(copy.start)
                else:
                    copy.start()

    def product(k, count, sl):
        left = rows[pl.ds(k, count), :, :, sl].reshape(count * ROWS, TILE)
        right = terms[pl.ds(k, count)].reshape(count * ROWS, 2 * HALF)
        return lax.dot_general(left, right, (((0,), (0,)), ((), ())), preferred_element_type=F32)

    def tile(i):
        return pl.ds(pl.multiple_of(i * TILE, TILE), TILE)

    def accumulate(k, count):
        @pl.loop(0, D // TILE)
        def _(i):
            acc[tile(i), :] += product(k, count, tile(i))

    @pl.loop(0, STEPS)
    def _(k):
        step(k)

        @pl.when((k == 1) | (k == 3) | (k == 5))
        def _():
            accumulate(k - 1, 2)

        @pl.when(k == 6)
        def _():
            accumulate(6, 1)

    def out_copies(i, b):
        return (
            pltpu.make_async_copy(stage.at[b, :, pl.ds(0, HALF)], gg_hbm.at[0, tile(i), :], out_sem.at[b, 0]),
            pltpu.make_async_copy(stage.at[b, :, pl.ds(HALF, HALF)], gu_hbm.at[0, tile(i), :], out_sem.at[b, 1]),
        )

    @pl.loop(0, D // TILE)
    def _(i):
        b = i % 2

        @pl.when(i >= 2)
        def _():
            for copy in out_copies(i - 2, b):
                copy.wait()

        stage[b] = (acc[tile(i), :] + product(STEPS - 1, 1, tile(i))).astype(BF16)
        for copy in out_copies(i, b):
            copy.start()

    @pl.loop(1, N_EXP)
    def _(i):
        pltpu.make_async_remote_copy(
            ret_out.at[0], ret_own.at[i], rets_sem.at[0], retr_sem.at[i], device_id=partner, device_id_type=MESH).wait_recv()

    self_ret.wait()
    ret_forward = pltpu.make_async_remote_copy(
        ret_own, ret_part, part_sem.at[2], part_sem.at[3], device_id=partner, device_id_type=MESH)
    ret_forward.start()
    ret_forward.wait_recv()
    sums = jnp.where(g == 0, ret_own[:, 0, :] + ret_part[:, 0, :], ret_own[:, 1, :] + ret_part[:, 1, :])
    by_slot = lax.dot_general(
        sums, member_ref[...], (((0,), (0,)), ((), ())), precision=HIGH, preferred_element_type=F32)
    pg_ref[...] = jnp.sum(jnp.where(lane_slot == pos, by_slot, 0.0), axis=0, keepdims=True)

    for i in (D // TILE - 2, D // TILE - 1):
        for copy in out_copies(i, i % 2):
            copy.wait()
    prob_forward.wait_send()
    ret_forward.wait_send()

    @pl.loop(1, N_EXP)
    def _(i):
        k, m, dx = i // 8, (i // 4) % 2, i % 4
        send_copy(k, m, dx).wait_send()
        prob_copy(k, m, dx).wait_send()

    @pl.loop(0, N_EXP)
    def _(i):
        k, m, s = i // 8, (i // 4) % 2, i % 4

        @pl.when((i >= 4) | (s != x))
        def _():
            return_copy(k, m, s).wait_send()

    @pl.loop(0, STEPS)
    def _(k):
        forward_copy(k).wait_send()


def body(tokens, routes, gate_prob, w_gate, w_up, hidden_grad):
    hbm = pl.BlockSpec(memory_space=pl.ANY)
    vmem = pl.BlockSpec(memory_space=pltpu.VMEM)
    dma = pltpu.SemaphoreType.DMA
    grad = jax.ShapeDtypeStruct((1, D, HALF), BF16)
    grad_gate, grad_up, prob_grad = pl.pallas_call(
        kernel,
        out_shape=(grad, grad, jax.ShapeDtypeStruct((1, TOK), F32)),
        in_specs=[hbm, vmem, vmem, hbm, hbm, hbm],
        out_specs=(hbm, hbm, vmem),
        scratch_shapes=[
            pltpu.VMEM((TOK, D), BF16),
            pltpu.VMEM((N_EXP, 16, MAIN), BF16),
            pltpu.VMEM((N_EXP, 16, MAIN), BF16),
            pltpu.VMEM((STEPS, 2, 2 * GROUP, D), BF16),
            pltpu.VMEM((D, HALF), BF16),
            pltpu.VMEM((D, HALF), BF16),
            pltpu.VMEM((1536, HALF), BF16),
            pltpu.VMEM((D, 2 * HALF), F32),
            pltpu.VMEM((STEPS, ROWS, 2 * HALF), BF16),
            pltpu.VMEM((2, TILE, 2 * HALF), BF16),
            pltpu.VMEM((N_EXP, TOK), F32),
            pltpu.VMEM((N_EXP, 1, 128), F32),
            pltpu.VMEM((N_EXP, 1, 128), F32),
            pltpu.VMEM((N_EXP, 1, 128), F32),
            pltpu.VMEM((N_EXP, 2, 128), F32),
            pltpu.VMEM((N_EXP, 2, 128), F32),
            pltpu.VMEM((N_EXP, 2, 128), F32),
            dma((N_EXP,)), dma((N_EXP,)), dma((N_EXP,)), dma((N_EXP,)), dma((N_EXP,)), dma((N_EXP,)),
            dma((STEPS,)), dma((STEPS,)), dma((4,)), dma((7,)), dma((2, 2)), dma((3,)),
        ],
        compiler_params=pltpu.CompilerParams(
            collective_id=0, has_side_effects=True, vmem_limit_bytes=63 * 1024 * 1024),
        cost_estimate=pl.CostEstimate(flops=26 * 10**9, bytes_accessed=20 * 10**6, transcendentals=10**6),
        name="moe_grads",
    )(tokens, routes.reshape(1, TOK), gate_prob.reshape(1, TOK), w_gate, w_up, hidden_grad)
    return grad_gate, grad_up, prob_grad.reshape(TOK, 1)


def solution(mesh):
    in_specs = (
        P(("exp", "grp"), None),
        P(("exp", "grp"), None),
        P(("exp", "grp"), None),
        P("exp", None, "grp"),
        P("exp", None, "grp"),
        P("exp", None, "grp"),
    )
    out_specs = (P("exp", None, "grp"), P("exp", None, "grp"), P(("exp", "grp"), None))
    return jax.shard_map(body, mesh=mesh, in_specs=in_specs, out_specs=out_specs, check_vma=False)
```

time: 253 us -> 124 us (0.49)
  blocking collectives: 135 us -> 0 us
  Pallas kernels: 0 us -> 116 us
  matrix products: 52.1 us -> 0 us
  waiting for transfers between devices: 21.7 us -> 0 us
  local copies, waits for them, and re-layouts: 22.6 us -> 6.7 us
  between operations: 14.8 us -> 0.65 us
  other arithmetic: 5.31 us -> 0 us
    all_to_all x3 -> x0, blocking collectives: 128 us -> none  [the longest x1 97.2 us: body(): lax.all_to_all(send_rows, 'exp', split_axis=0, concat_axis=0, tiled=True)]
    pallas_call x0 -> x1, Pallas kernels: none -> 116 us  [body(): pl.pallas_call(kernel, out_shape=(grad, grad, jax.ShapeDtypeStruct((1, TO...]
    dot_general x5 -> x0, matrix products: 52.1 us -> none  [the longest x1 12.4 us: finish_slots(): lax.dot_general(rows, up_term, contract, preferred_element_type=jnp.float32)]
    all_gather x1 -> x0, waiting for transfers between devices: 21.7 us -> none  [body(): lax.all_gather(local_rows, 'grp', axis=0, tiled=True)]
    reshape x2 -> x0, local copies, waits for them, and re-layouts: 18.6 us -> none  [the longest x1 9.38 us: body(): local_rows = arrived_rows.reshape(expert_count * capacity, features)]
    all_gather x1 -> x0, blocking collectives: 4.54 us -> none  [body(): lax.all_gather(local_prob, 'grp', axis=0, tiled=True)]
    unnamed x16 -> x7, local copies, waits for them, and re-layouts: 2.87 us -> 6.7 us
  transfers between devices with their start and end apart: 1 -> 0, of which waited for: 1 -> 0; matrix products, arithmetic and copies ran while one was open for 1% -> 0% of each run, Pallas kernels for 0% -> 0%
where the time goes in v1:
time: 124 us
  Pallas kernels  116 us (94%)
  local copies, waits for them, and re-layouts  6.7 us (5%)
    pallas_call x1, Pallas kernels, body(): pl.pallas_call(kernel, out_shape=(grad, grad, jax.ShapeDtypeStruct((1, TO...  116 us
    unnamed x7, local copies, waits for them, and re-layouts  6.7 us

profile of v1, /device:TPU:1, one launch (start us, length us, event | category | flops | bytes accessed | tf_op | source)
XLA Modules:
  0.0 123.6 jit_solution(3902072858576409786)
XLA Ops:
  0.6 116.3 %moe_grads.1 = (bf16[1,3584,512]{2,1,0:T(8,128)(2,1)}, bf16[1,3584,512]{2,1,0:T(8,128)(2,1)}, f32[1,512]{1,0:T(1,128)}) custom-call(bf16[512,3584]{1,0:T(8,128)(2,1)} %tok_hbm.1, s32[1,512]{1,0:T(1,128)} %bitcast.4, f32[1,512]{1,0:T(1,128)} %bitcast.5, bf16[1,3584,512]{2,1,0:T(8,128)(2,1)} %wg_hbm.1, bf16[1,3584,512]{2,1,0:T(8,128)(2,1)} %wu_hbm.1, ...), custom_call_target="tpu_custom_call" | custom-call | flops 25999998976 | bytes 20000000 | tf_op jit(solution)/shard_map/moe_grads/pallas_call | solution.py:349
  116.9 0.0 copy-start
  116.9 4.3 %copy.12 = bf16[1,3584,512]{2,1,0:T(8,128)(2,1)} copy(bf16[1,3584,512]{2,1,0:T(8,128)(2,1)} %get-tuple-element.12) | data formatting | bytes 7340032
  121.2 0.0 copy-done
  121.2 0.0 copy-start.1
  121.2 1.8 %copy.13 = bf16[1,3584,512]{2,1,0:T(8,128)(2,1)} copy(bf16[1,3584,512]{2,1,0:T(8,128)(2,1)S(1)} %copy-done) | data formatting | bytes 7340032
  123.0 0.0 copy-done.1
  123.0 0.6 copy.14
Async XLA Ops:
  116.9 4.3 %copy-start = (bf16[1,3584,512]{2,1,0:T(8,128)(2,1)S(1)}, bf16[1,3584,512]{2,1,0:T(8,128)(2,1)}, u32[]{:S(2)}) copy-start(bf16[1,3584,512]{2,1,0:T(8,128)(2,1)} %get-tuple-element.13) | copy-start | bytes 11010052
  121.2 1.8 %copy-start.1 = (f32[1,512]{1,0:T(1,128)S(1)}, f32[1,512]{1,0:T(1,128)}, u32[]{:S(2)}) copy-start(f32[1,512]{1,0:T(1,128)} %get-tuple-element.8) | copy-start | bytes 6148

commit v2 on v1

v2 whole, which is shorter than its diff:
```python
import jax
import jax.numpy as jnp
from jax import lax
from jax.experimental import pallas as pl
from jax.experimental.pallas import tpu as pltpu
from jax.sharding import PartitionSpec as P

BF16, F32, I32 = jnp.bfloat16, jnp.float32, jnp.int32
MESH = pl.DeviceIdType.MESH
HIGH = lax.Precision.HIGHEST

D = 3584
HALF = 512
TOK = 512
N_EXP = 64
CAP = 12
PART = 896
MAIN = 3 * PART
STEPS = 8
ROWS = 192
GROUP = 48
TILE = 896
AHEAD = 3
CHUNKS = ((0, 8), (8, 16), (24, 40))


def kernel(
    tok_hbm, routes_ref, prob_ref, wg_hbm, wu_hbm, hg_hbm,
    gg_ref, gu_ref, pg_ref,
    tok, send, recv, rows, wg, wu, hg, terms, member_ref,
    prs, pr_own, pr_part, ret_out, ret_own,
    send_sem, recv_sem, prs_sem, prr_sem, rets_sem, retr_sem,
    fwds_sem, fwdr_sem, pfs_sem, pfr_sem, load_sem, self_sem,
):
    me = lax.axis_index("exp")
    g = lax.axis_index("grp")
    z, y, x = lax.div(me, 16), lax.rem(lax.div(me, 4), 4), lax.rem(me, 4)
    partner = {"exp": me, "grp": 1 - g}
    zs = [lax.rem(z + d, 4) * 16 for d in range(4)]
    ys = [lax.rem(y + d, 4) * 4 for d in range(4)]
    xs = [lax.rem(x + d, 4) for d in range(4)]

    def target(k, m, dx):
        return zs[(k // 4 + 2 * m) % 4] + ys[(k % 4 + 2 * m) % 4] + xs[dx]

    def send_step(k):
        slot, group = [], []
        for m in range(2):
            dz, dy = lax.div(k, 4) + 2 * m, lax.rem(k, 4) + 2 * m
            group.append(lax.rem(z + dz, 4) * 16 + lax.rem(y + dy, 4) * 4)
            slot.append((k * 2 + m) * 4 + x)
        for i in range(8):
            m = i % 2
            dx = (i // 2 + 2 * m) % 4
            pltpu.make_async_remote_copy(
                send.at[k * 8 + m * 4 + dx], recv.at[slot[m]], send_sem, recv_sem.at[k * 2 + m],
                device_id={"exp": group[m] + xs[dx], "grp": g}, device_id_type=MESH).start()
            pltpu.make_async_remote_copy(
                prs.at[k * 8 + m * 4 + dx], pr_own.at[slot[m]], prs_sem, prr_sem.at[k],
                device_id={"exp": group[m] + xs[dx], "grp": g}, device_id_type=MESH).start()

    def group_of(k, m):
        dz, dy = lax.div(k, 4) + 2 * m, lax.rem(k, 4) + 2 * m
        return lax.rem(z + 8 - dz, 4) * 4 + lax.rem(y + 8 - dy, 4)

    def columns(p):
        return pl.ds(p * PART, PART)

    tok_loads = [pltpu.make_async_copy(tok_hbm.at[:, columns(p)], tok.at[:, columns(p)], load_sem.at[p]) for p in range(4)]
    for p in (3, 0, 1, 2):
        tok_loads[p].start()
    barrier = pltpu.get_barrier_semaphore()
    for i in range(1, N_EXP):
        pl.semaphore_signal(
            barrier, inc=1, device_id={"exp": target(i // 8, (i // 4) % 2, i % 4), "grp": g}, device_id_type=MESH)

    pl.semaphore_signal(barrier, inc=1, device_id=partner, device_id_type=MESH)

    w_loads = [
        pltpu.make_async_copy(wg_hbm.at[0], wg, load_sem.at[4]),
        pltpu.make_async_copy(wu_hbm.at[0], wu, load_sem.at[5]),
        pltpu.make_async_copy(hg_hbm.at[0], hg, load_sem.at[6]),
    ]
    for load in w_loads:
        load.start()

    r = lax.broadcasted_iota(I32, (N_EXP, TOK), 0)
    rk, rm, rx = r >> 3, (r >> 2) & 1, r & 3
    expert = ((z + (rk >> 2) + 2 * rm) & 3) * 16 + ((y + (rk & 3) + 2 * rm) & 3) * 4 + ((x + rx) & 3)
    member = jnp.where(expert == routes_ref[...], 1.0, 0.0).astype(F32)
    member_ref[...] = member
    before = lax.broadcasted_iota(I32, (TOK, TOK), 0) < lax.broadcasted_iota(I32, (TOK, TOK), 1)
    earlier = jnp.dot(member.astype(BF16), jnp.where(before, 1.0, 0.0).astype(BF16), preferred_element_type=F32)
    pos = jnp.sum(member * earlier, axis=0, keepdims=True).astype(I32)
    rank = jnp.sum(member * r.astype(F32), axis=0, keepdims=True).astype(I32)
    main_row = rank * 16 + ((12 * x + pos) & 15)
    tail_row = rank * 8 + (pos & 3)
    tail_part = pos >> 2
    tail_first = (12 * x + 12) % 16
    i16 = lax.broadcasted_iota(I32, (1, 16, PART), 1)
    tail_mask = (i16 >= tail_first) & (i16 < tail_first + 4)

    lane_slot = lax.broadcasted_iota(I32, (128, TOK), 0)
    prob_at = jnp.where(lane_slot == pos, prob_ref[...], 0.0).astype(BF16)
    prs[:, 0, :] = lax.dot_general(member.astype(BF16), prob_at, (((1,), (1,)), ((), ())), preferred_element_type=F32)

    def send_copy(k, m, dx):
        rk_ = k * 8 + m * 4 + dx
        slot = (k * 2 + m) * 4 + x
        return pltpu.make_async_remote_copy(
            send.at[rk_], recv.at[slot], send_sem, recv_sem.at[k * 2 + m],
            device_id={"exp": target(k, m, dx), "grp": g}, device_id_type=MESH)

    def prob_copy(k, m, dx):
        rk_ = k * 8 + m * 4 + dx
        slot = (k * 2 + m) * 4 + x
        return pltpu.make_async_remote_copy(
            prs.at[rk_], pr_own.at[slot], prs_sem, prr_sem.at[k],
            device_id={"exp": target(k, m, dx), "grp": g}, device_id_type=MESH)

    def return_copy(k, m, sx, group, j):
        slot = g * N_EXP + k * 8 + m * 4 + xs[(4 - sx) % 4]
        return pltpu.make_async_remote_copy(
            ret_out.at[j * N_EXP + k * 8 + m * 4 + sx], ret_own.at[slot], rets_sem, retr_sem,
            device_id={"exp": group * 4 + sx, "grp": j}, device_id_type=MESH)

    def peers_copy(source, landing, first, out_sem_, in_sem_, count=N_EXP - 1):
        return pltpu.make_async_remote_copy(
            source.at[pl.ds(first, count)], landing.at[pl.ds(first, count)], out_sem_, in_sem_,
            device_id=partner, device_id_type=MESH)

    self_rows = pltpu.make_async_copy(send.at[0], recv.at[x], self_sem.at[0])
    self_prob = pltpu.make_async_copy(prs.at[0], pr_own.at[x], self_sem.at[1])
    self_ret = pltpu.make_async_copy(ret_out.at[g * N_EXP + x], ret_own.at[g * N_EXP], self_sem.at[2])

    def build(first, count):
        hit = lax.broadcasted_iota(I32, (16 * count, TOK), 0) + 16 * first == main_row
        pick = jnp.where(hit, 1.0, 0.0).astype(BF16)
        it = lax.broadcasted_iota(I32, (8 * count, TOK), 0) + 8 * first
        picks = []
        for p in range(3):
            own = jnp.where(tail_part == p, tail_row, -100)
            picks.append(jnp.where((it == own) | (it == own + 4), 1.0, 0.0).astype(BF16))
        if first == 0:
            tok_loads[3].wait()
        tails = jnp.dot(jnp.concatenate(picks, axis=0), tok[:, MAIN:], preferred_element_type=F32)
        for p in range(3):
            if first == 0:
                tok_loads[p].wait()
            main = jnp.dot(pick, tok[:, p * PART:(p + 1) * PART], preferred_element_type=F32)
            tail = tails[p * 8 * count:(p + 1) * 8 * count].reshape(count, 8, PART)
            both = jnp.concatenate([tail, tail], axis=1)
            block = jnp.where(tail_mask, both, main.reshape(count, 16, PART)).astype(BF16)
            send[first:first + count, :, p * PART:(p + 1) * PART] = block

    for first, count in CHUNKS:
        build(first, count)
        if first == 0:
            pl.semaphore_wait(barrier, N_EXP)
            self_rows.start()
            self_prob.start()

        for i in range(max(first, 1), min(first + count, 8 * AHEAD)):
            send_copy(i // 8, i % 2, ((i % 8) // 2 + 2 * (i % 2)) % 4).start()
            prob_copy(i // 8, i % 2, ((i % 8) // 2 + 2 * (i % 2)) % 4).start()

    for load in w_loads:
        load.wait()

    def forward_copy(k):
        return pltpu.make_async_remote_copy(
            rows.at[k, g], rows.at[k, g], fwds_sem.at[k], fwdr_sem.at[k], device_id=partner, device_id_type=MESH)

    def prob_forward(k):
        part = pl.ds(k * 8, 8)
        return pltpu.make_async_remote_copy(
            pr_own.at[part], pr_part.at[part], pfs_sem.at[k], pfr_sem.at[k], device_id=partner, device_id_type=MESH)

    low = lax.broadcasted_iota(I32, (8, PART), 0) < 4

    def unpack(k, m):
        base = (k * 2 + m) * 4

        def half(s, h, p):
            return recv[base + s, :, p * PART:(p + 1) * PART].astype(F32)[8 * h:8 * h + 8]

        def put(t, p, lo, hi):
            rows[k, g, m * GROUP + 16 * t:m * GROUP + 16 * t + 16, p * PART:(p + 1) * PART] = jnp.concatenate(
                [lo, hi], axis=0).astype(BF16)

        for p in range(3):
            put(0, p, half(0, 0, p), jnp.where(low, half(0, 1, p), half(1, 1, p)))
            put(1, p, half(1, 0, p), half(2, 1, p))
            put(2, p, jnp.where(low, half(2, 0, p), half(3, 0, p)), half(3, 1, p))

        def quad(q):
            s, p = q // 3, q % 3
            at = 3 - s
            value = half(s, at // 2, p)
            return value if at % 2 == q % 2 else pltpu.roll(value, 4, 0)

        for t in range(3):
            lo, hi = (jnp.where(low, quad(4 * t + 2 * h), quad(4 * t + 2 * h + 1)) for h in range(2))
            put(t, 3, lo, hi)

    row16 = lax.broadcasted_iota(I32, (ROWS, 16), 0)
    at16 = lax.broadcasted_iota(I32, (ROWS, 16), 1) * CAP
    spread = jnp.where((row16 >= at16) & (row16 < at16 + CAP), 1.0, 0.0)
    row_t = lax.broadcasted_iota(I32, (16, ROWS), 1)
    at_t = lax.broadcasted_iota(I32, (16, ROWS), 0) * CAP
    spread_t = jnp.where((row_t >= at_t) & (row_t < at_t + CAP), 1.0, 0.0)
    row128 = lax.broadcasted_iota(I32, (ROWS, 128), 0)
    lane_hit = lax.broadcasted_iota(I32, (ROWS, 128), 1) == row128 - ((row128 * 5462) >> 16) * CAP

    def product(k, count, sl):
        left = rows[pl.ds(k, count), :, :, sl].reshape(count * ROWS, TILE)
        right = terms[pl.ds(k, count)].reshape(count * ROWS, 2 * HALF)
        return lax.dot_general(left, right, (((0,), (0,)), ((), ())), preferred_element_type=F32)

    def tile(i):
        return pl.ds(pl.multiple_of(i * TILE, TILE), TILE)

    def put_grads(i, value, add):
        for ref, half in ((gg_ref, value[:, :HALF]), (gu_ref, value[:, HALF:])):
            if add:
                half = half + ref[0, tile(i), :].astype(F32)
            ref[0, tile(i), :] = half.astype(BF16)

    def accumulate(k):
        odd = lax.rem(k, 2)
        first_tile, last_tile = 2 * odd, 2 + 2 * odd

        @pl.when((k == 4) | (k == 5))
        def _():
            @pl.loop(first_tile, last_tile)
            def _(i):
                put_grads(i, product(0, 4, tile(i)), False)

        @pl.when(k >= 6)
        def _():
            @pl.loop(first_tile, last_tile)
            def _(i):
                put_grads(i, product(4, 2, tile(i)), True)

    def step(k):
        first = k == 0

        @pl.when(first)
        def _():
            peers_copy(send, recv, 0, send_sem, recv_sem.at[0], 3).wait_recv()
            peers_copy(prs, pr_own, 0, prs_sem, prr_sem.at[0], 7).wait_recv()
            self_rows.wait()
            self_prob.wait()

        @pl.when(jnp.logical_not(first))
        def _():
            peers_copy(send, recv, 0, send_sem, recv_sem.at[2 * k], 4).wait_recv()
            peers_copy(prs, pr_own, 0, prs_sem, prr_sem.at[k], 8).wait_recv()

        peers_copy(send, recv, 0, send_sem, recv_sem.at[2 * k + 1], 4).wait_recv()

        @pl.when(k < STEPS - AHEAD)
        def _():
            send_step(k + AHEAD)

        groups = [group_of(k, 0), group_of(k, 1)]
        prob_forward(k).start()
        unpack(k, 0)
        unpack(k, 1)
        forward = forward_copy(k)
        forward.start()

        accumulate(k)

        prob_forward(k).wait_recv()
        own_p, other_p = pr_own[pl.ds(k * 8, 8), 0, :], pr_part[pl.ds(k * 8, 8), 0, :]
        mine = g == 0
        probs = jnp.concatenate([jnp.where(mine, own_p, other_p), jnp.where(mine, other_p, own_p)], axis=0)
        probs = jnp.dot(spread.astype(BF16), probs.astype(BF16), preferred_element_type=F32)
        prob = jnp.sum(jnp.where(lane_hit, probs, 0.0), axis=1, keepdims=True)
        forward.wait_recv()

        total = jnp.zeros((ROWS, 1), F32)
        width = 256
        for n in range(HALF // width):
            sl = slice(n * width, (n + 1) * width)
            here = rows[k].reshape(ROWS, D)
            gate = jnp.dot(here, wg[:, sl], preferred_element_type=F32)
            up = jnp.dot(here, wu[:, sl], preferred_element_type=F32)
            pieces = [
                hg[pl.ds(pl.multiple_of(j * 768 + groups[m] * GROUP, 16), GROUP), sl] for j in range(2) for m in range(2)]
            cot = jnp.concatenate(pieces, axis=0).astype(F32)
            sig = jax.nn.sigmoid(gate)
            act = gate * sig
            total = total + jnp.sum(act * up * cot, axis=1, keepdims=True)
            scaled = prob * cot
            terms[k, :, sl] = (scaled * up * sig * (1.0 + gate * (1.0 - sig))).astype(BF16)
            terms[k, :, HALF + n * width:HALF + (n + 1) * width] = (scaled * act).astype(BF16)
        by_source = jnp.dot(
            spread_t, jnp.where(lane_hit, total, 0.0), precision=HIGH, preferred_element_type=F32)
        for j in range(2):
            ret_out[pl.ds(j * N_EXP + k * 8, 8), 0, :] = by_source[8 * j:8 * j + 8]
        for m in range(2):
            for s in range(4):
                for j in range(2):
                    copy = return_copy(k, m, s, groups[m], j)
                    if m == 0:
                        own = (k == 0) & (x == s) & (g == j)
                        pl.when(own)(self_ret.start)
                        pl.when(jnp.logical_not(own))(copy.start)
                    else:
                        copy.start()

    @pl.loop(0, STEPS)
    def _(k):
        step(k)

    @pl.loop(0, D // TILE)
    def _(i):
        put_grads(i, product(STEPS - 2, 2, tile(i)), True)

    peers_copy(ret_out, ret_own, 0, rets_sem, retr_sem, 2 * N_EXP - 1).wait_recv()
    self_ret.wait()
    sums = ret_own[0:N_EXP, 0, :] + ret_own[N_EXP:, 0, :]
    by_slot = lax.dot_general(
        sums, member_ref[...], (((0,), (0,)), ((), ())), precision=HIGH, preferred_element_type=F32)
    pg_ref[...] = jnp.sum(jnp.where(lane_slot == pos, by_slot, 0.0), axis=0, keepdims=True)

    peers_copy(send, recv, 0, send_sem, recv_sem.at[0]).wait_send()
    peers_copy(prs, pr_own, 0, prs_sem, prr_sem.at[0]).wait_send()
    peers_copy(ret_out, ret_own, 0, rets_sem, retr_sem, 2 * N_EXP - 1).wait_send()

    @pl.loop(0, STEPS)
    def _(k):
        forward_copy(k).wait_send()
        prob_forward(k).wait_send()


def body(tokens, routes, gate_prob, w_gate, w_up, hidden_grad):
    hbm = pl.BlockSpec(memory_space=pl.ANY)
    vmem = pl.BlockSpec(memory_space=pltpu.VMEM)
    dma = pltpu.SemaphoreType.DMA
    grad = pltpu.VMEM((1, D, HALF), BF16)
    grad_gate, grad_up, prob_grad = pl.pallas_call(
        kernel,
        out_shape=(grad, grad, jax.ShapeDtypeStruct((1, TOK), F32)),
        in_specs=[hbm, vmem, vmem, hbm, hbm, hbm],
        out_specs=(vmem, vmem, vmem),
        scratch_shapes=[
            pltpu.VMEM((TOK, D), BF16),
            pltpu.VMEM((N_EXP, 16, MAIN), BF16),
            pltpu.VMEM((N_EXP, 16, MAIN), BF16),
            pltpu.VMEM((STEPS, 2, 2 * GROUP, D), BF16),
            pltpu.VMEM((D, HALF), BF16),
            pltpu.VMEM((D, HALF), BF16),
            pltpu.VMEM((1536, HALF), BF16),
            pltpu.VMEM((STEPS, ROWS, 2 * HALF), BF16),
            pltpu.VMEM((N_EXP, TOK), F32),
            pltpu.VMEM((N_EXP, 1, 128), F32),
            pltpu.VMEM((N_EXP, 1, 128), F32),
            pltpu.VMEM((N_EXP, 1, 128), F32),
            pltpu.VMEM((2 * N_EXP, 1, 128), F32),
            pltpu.VMEM((2 * N_EXP, 1, 128), F32),
            dma, dma((2 * STEPS,)), dma, dma((STEPS,)), dma, dma,
            dma((STEPS,)), dma((STEPS,)), dma((STEPS,)), dma((STEPS,)), dma((7,)), dma((3,)),
        ],
        compiler_params=pltpu.CompilerParams(
            collective_id=0, has_side_effects=True, vmem_limit_bytes=54 * 1024 * 1024),
        cost_estimate=pl.CostEstimate(flops=26 * 10**9, bytes_accessed=20 * 10**6, transcendentals=10**6),
        name="moe_grads",
    )(tokens, routes.reshape(1, TOK), gate_prob.reshape(1, TOK), w_gate, w_up, hidden_grad)
    return grad_gate, grad_up, prob_grad.reshape(TOK, 1)


def solution(mesh):
    in_specs = (
        P(("exp", "grp"), None),
        P(("exp", "grp"), None),
        P(("exp", "grp"), None),
        P("exp", None, "grp"),
        P("exp", None, "grp"),
        P("exp", None, "grp"),
    )
    out_specs = (P("exp", None, "grp"), P("exp", None, "grp"), P(("exp", "grp"), None))
    return jax.shard_map(body, mesh=mesh, in_specs=in_specs, out_specs=out_specs, check_vma=False)
```

time: 124 us -> 104 us (0.84)
  the two profiles are of different devices: /device:TPU:1 before, /device:TPU:25 now
where the time goes in v2:
time: 104 us; the launch traced here: 103 us
  Pallas kernels  98.5 us (95%)
  local copies, waits for them, and re-layouts  4.26 us (4%)
    pallas_call x1, Pallas kernels, body(): pl.pallas_call(kernel, out_shape=(grad, grad, jax.ShapeDtypeStruct((1, TO...  98.5 us
    unnamed x5, local copies, waits for them, and re-layouts  4.26 us

profile of v2, /device:TPU:25, one launch (start us, length us, event | category | flops | bytes accessed | tf_op | source)
XLA Modules:
  0.0 103.4 jit_solution(5814851271022823998)
XLA Ops:
  0.6 98.5 %moe_grads.1 = (bf16[1,3584,512]{2,1,0:T(8,128)(2,1)S(1)}, bf16[1,3584,512]{2,1,0:T(8,128)(2,1)S(1)}, f32[1,512]{1,0:T(1,128)}) custom-call(bf16[512,3584]{1,0:T(8,128)(2,1)} %tok_hbm.1, s32[1,512]{1,0:T(1,128)} %bitcast.4, f32[1,512]{1,0:T(1,128)} %bitcast.5, bf16[1,3584,512]{2,1,0:T(8,128)(2,1)} %wg_hbm.1, bf16[1,3584,512]{2,1,0:T(8,128)(2,1)} %wu_hbm.1, ...), custom_call_target="tpu_custom_call" | custom-call | flops 25999998976 | bytes 20000000 | tf_op jit(solution)/shard_map/moe_grads/pallas_call | solution.py:344
  99.2 1.8 %copy.12 = bf16[1,3584,512]{2,1,0:T(8,128)(2,1)} copy(bf16[1,3584,512]{2,1,0:T(8,128)(2,1)S(1)} %get-tuple-element.9) | data formatting | bytes 7340032
  101.0 0.0 copy-start
  101.0 1.8 %copy.13 = bf16[1,3584,512]{2,1,0:T(8,128)(2,1)} copy(bf16[1,3584,512]{2,1,0:T(8,128)(2,1)S(1)} %get-tuple-element.10) | data formatting | bytes 7340032
  102.8 0.0 copy-done
  102.8 0.6 copy.14
Async XLA Ops:
  101.0 1.8 %copy-start = (f32[1,512]{1,0:T(1,128)S(1)}, f32[1,512]{1,0:T(1,128)}, u32[]{:S(2)}) copy-start(f32[1,512]{1,0:T(1,128)} %get-tuple-element.8) | copy-start | bytes 6148
